TPU v7x, 32 devices: a whole 2x2x4 slice. The times are simulated.
32 devices in a mesh: sec: 8 (over y, x, core), span: 4 (over z).
Axes of the slice: x: 2, y: 2, z: 4, core: 2. Of those that a mesh axis runs over, the one named last changes fastest.
Arguments:
- density: float32 [192, 1024], P('sec', 'span'), may hold values from 0.5 to 2
- fields: float32 [4, 192, 1024], P(None, 'sec', 'span'), may hold values from -6 to 6
- bins: int32 [192, 1024], P('sec', 'span'), may hold values from 0 to 127
- owner: int32 [192], P('sec'), may hold values from 0 to 31
- species: float32 [32, 32, 128], P(('sec', 'span')), may hold values from -6 to 6
- rate_matrix: float32 [32, 32], replicated, may hold values from -1 to 1
- inv_weight: float32 [32], replicated, may hold values from 0.5 to 2
- formation: float32 [32], replicated, may hold values from -4 to 4
Outputs:
- species_out: float32 [32, 32, 128], P(('sec', 'span'))
- density_out: float32 [192, 1024], P('sec', 'span')
- fields_out: float32 [4, 192, 1024], P(None, 'sec', 'span')
All inputs are finite; a program needn't handle non-finite values.
Results may differ from a plain program's by a relative error of at most 0.0003.
Values sent between devices are 32-bit elements; how exact they have to be, the bound alone decides.
A program may use at most 64 MiB of HBM per device.

v0:
```python
import math

import jax
import jax.numpy as jnp
from jax import lax
from jax.sharding import PartitionSpec as P

COUPLING = 2


def from_behind(value, axis, steps):
    count = lax.axis_size(axis)
    first, last = (max(0, -steps), min(count, count - steps))
    return lax.ppermute(value, axis, [(source, source + steps) for source in range(first, last)])


def extended_2(shard, sides, width):
    for axis, dim in sides:
        count, length = (lax.axis_size(axis), shard.shape[dim])
        up = [(i, (i + 1) % count) for i in range(count)]
        down = [(j, i) for i, j in up]
        last = lax.slice_in_dim(shard, length - width, length, axis=dim)
        first = lax.slice_in_dim(shard, 0, width, axis=dim)
        before = lax.ppermute(last, axis, up)
        after = lax.ppermute(first, axis, down)
        shard = jnp.concatenate([before, shard, after], axis=dim)
    return shard


def column_sums(values, bins, nbins):
    cols, quant, zlen = values.shape
    block = math.gcd(cols, 16)
    value_blocks = values.reshape(cols // block, block, quant, zlen)
    bin_blocks = bins.reshape(cols // block, block, zlen)

    def one_block(pair):
        vals, labels = pair
        hot = (labels[:, :, None] == jnp.arange(nbins, dtype=jnp.int32)).astype(jnp.float32)
        return jnp.einsum("cqz,czb->cqb", vals, hot, precision=lax.Precision.HIGHEST)

    out = lax.map(one_block, (value_blocks, bin_blocks))
    return out.reshape(cols, quant * nbins)


def body(density, fields, bins, owner, species, rate_matrix, inv_weight, formation):
    nbins = species.shape[2]
    nspec = species.shape[1]
    sections = lax.axis_size("sec") * lax.axis_size("span")
    eta = (jnp.arange(nbins, dtype=jnp.float32) + 0.5) / nbins
    index = owner[:, None] * nbins + bins
    for step in range(COUPLING):
        values = jnp.stack([density] + [density * fields[k] for k in range(4)], axis=1)
        hist = column_sums(values, bins, nbins)
        hot = (owner[:, None] == jnp.arange(sections, dtype=jnp.int32)[None, :]).astype(jnp.float32)
        grouped = lax.psum_scatter(
            lax.dot_general(
                hot,
                hist,
                (((0,), (0,)), ((), ())),
                precision=lax.Precision.HIGHEST,
                preferred_element_type=jnp.float32,
            ),
            "sec",
            scatter_dimension=0,
            tiled=True,
        )
        own = lax.psum_scatter(grouped, "span", scatter_dimension=0, tiled=True)
        own = own.reshape(5, nbins)
        weight = jnp.maximum(own[0], 1.0)
        cond = own[1:] / weight[None]
        current = species[0]
        before = from_behind(species, ("sec", "span"), 1)[0]
        temp = 1.0 + 4.0 * eta * (1.0 - eta) + 0.5 * jnp.tanh(cond[2])
        rate = jnp.exp(2.0 * (1.0 - 1.0 / temp))
        react = (
            jnp.dot(
                rate_matrix,
                current,
                precision=lax.Precision.HIGHEST,
                preferred_element_type=jnp.float32,
            )
            * rate[None, :]
        )
        padded = jnp.pad(current, ((0, 0), (1, 1)))
        lap = padded[:, 2:] + padded[:, :-2] - 2.0 * current
        mixing = 0.2 * jax.nn.sigmoid(cond[1])
        carried = 0.3 * jax.nn.sigmoid(cond[0])
        updated = (
            current + mixing[None, :] * lap - carried[None, :] * (current - before) + 0.2 * react
        )
        species = updated[None]
        mix = 1.0 + jnp.sum(inv_weight[:, None] * updated * updated, axis=0) / nspec
        rho_c = 1.0 / (temp * mix)
        temp_c = (
            temp
            + 0.1 * jnp.sum(formation[:, None] * react, axis=0)
            - 0.2 * jax.nn.sigmoid(cond[3]) * (temp - 0.5)
        )
        table = jnp.stack([rho_c, temp_c])[None]
        whole = lax.all_gather(table, ("sec", "span"), axis=0, tiled=True)
        rho_cell = whole[:, 0, :].reshape(-1)[index]
        temp_cell = whole[:, 1, :].reshape(-1)[index]
        extended = extended_2(fields, (("span", 2),), 1)
        lapz = extended[:, :, 2:] + extended[:, :, :-2] - 2.0 * fields
        fields = fields + 0.2 * lapz
        fields = fields.at[2].add(0.3 * (temp_cell - fields[2]))
        density = rho_cell
    return (species, density, fields)


def solution(mesh):
    return jax.shard_map(
        body,
        mesh=mesh,
        in_specs=(
            P("sec", "span"),
            P(None, "sec", "span"),
            P("sec", "span"),
            P("sec"),
            P(("sec", "span"), None, None),
            P(),
            P(),
            P(),
        ),
        out_specs=(P(("sec", "span"), None, None), P("sec", "span"), P(None, "sec", "span")),
        check_vma=False,
    )
```

profile of v0, /device:TPU:0, one launch (start us, length us, event | category | flops | bytes accessed | tf_op | source)
XLA Modules:
  0.0 438.5 jit_solution(10485076696519655297)
XLA Ops:
  8.0 0.8 bitcast_multiply_fusion
  9.9 2.4 while.22
  10.7 0.8 fusion.68
  11.6 0.8 fusion.68
  13.0 0.9 fusion.21
  14.7 4.9 %collective-permute-start = (f32[1,32,128]{2,1,0:T(8,128)S(1)}, f32[1,32,128]{2,1,0:T(8,128)S(1)}, u32[]{:S(2)}, u32[]{:S(2)}) collective-permute-start(f32[1,32,128]{2,1,0:T(8,128)S(1)} %copy-done.7), channel_id=1, source_target_pairs={{0,1},{1,2},{2,3},{3,4},{4,5},{5,6},{6,7},{7,8},{8,9},{9,10},{10,1... | collective-permute-start | bytes 49160 | tf_op jit(solution)/shard_map/ppermute | solution.py:14
  19.7 2.0 collective-permute-start.1
  24.4 3.7 collective-permute-done.2
  28.3 38.6 %all-reduce.9.cloned.1.call-done = f32[32,640]{1,0:T(8,128)} async-done(((f32[32,640]{1,0:T(8,128)}), f32[32,640]{1,0:T(8,128)}) %all-reduce.9.cloned.1.call-update) | async-done | bytes 81936
  67.6 18.7 %all-reduce.3 = f32[4,640]{1,0:T(4,128)S(1)} all-reduce(f32[4,640]{1,0:T(4,128)S(1)} %constant_dynamic-slice_fusion.3), channel_id=5, replica_groups=mesh['sec'=8,'span'=4] {'span'}, use_global_device_ids=true, to_apply=%region_3.4.clone | all-reduce | flops 2560 | bytes 20480
  88.6 63.5 %all-gather.2 = f32[32,2,128]{2,1,0:T(2,128)S(1)} all-gather(f32[1,2,128]{2,1,0:T(2,128)S(1)} %maximum_bitcast_fusion), channel_id=2, replica_groups=mesh['sec'=8,'span'=4] {'sec','span'}, dimensions={0}, use_global_device_ids=true | all-gather | bytes 33792 | tf_op jit(solution)/shard_map/all_gather | solution.py:100
  152.1 34.3 %gather_fusion.1 = f32[6144]{0:T(1024)S(1)} fusion(f32[4096]{0:T(1024)S(1)} %bitcast.134, s32[6144]{0:T(1024)S(1)} %broadcast_clamp_fusion), kind=kCustom, calls=%fused_computation.1 | custom fusion | bytes 73728 | tf_op jit(solution)/shard_map/gather | solution.py:102
  187.0 1.9 collective-permute-start.5
  188.9 34.3 %gather_fusion = f32[6144]{0:T(1024)S(1)} fusion(f32[4096]{0:T(1024)S(1)} %bitcast.132, s32[6144]{0:T(1024)S(1)} %broadcast_clamp_fusion), kind=kCustom, calls=%fused_computation | custom fusion | bytes 73728 | tf_op jit(solution)/shard_map/gather | solution.py:101
  223.5 2.5 while.23
  223.5 0.8 fusion.70
  225.2 0.8 fusion.70
  226.0 0.9 fusion.18
  227.0 3.9 collective-permute-start.3
  231.0 45.7 %all-reduce.11.cloned.1.call-done = f32[32,640]{1,0:T(8,128)} async-done(((f32[32,640]{1,0:T(8,128)}), f32[32,640]{1,0:T(8,128)}) %all-reduce.11.cloned.1.call-update) | async-done | bytes 81936
  277.4 18.7 %all-reduce.5 = f32[4,640]{1,0:T(4,128)S(1)} all-reduce(f32[4,640]{1,0:T(4,128)S(1)} %constant_dynamic-slice_fusion.1), channel_id=7, replica_groups=mesh['sec'=8,'span'=4] {'span'}, use_global_device_ids=true, to_apply=%region_9.10.clone | all-reduce | flops 2560 | bytes 20480
  298.3 63.5 %all-gather.3 = f32[32,2,128]{2,1,0:T(2,128)S(1)} all-gather(f32[1,2,128]{2,1,0:T(2,128)S(1)} %maximum_bitcast_fusion.1), channel_id=3, replica_groups=mesh['sec'=8,'span'=4] {'sec','span'}, dimensions={0}, use_global_device_ids=true | all-gather | bytes 33792 | tf_op jit(solution)/shard_map/all_gather | solution.py:100
  361.8 34.3 %gather_fusion.3 = f32[6144]{0:T(1024)S(1)} fusion(f32[4096]{0:T(1024)S(1)} %bitcast.135, s32[6144]{0:T(1024)S(1)} %broadcast_clamp_fusion), kind=kCustom, calls=%fused_computation.3 | custom fusion | bytes 73728 | tf_op jit(solution)/shard_map/gather | solution.py:102
  396.1 34.3 %gather_fusion.2 = f32[6144]{0:T(1024)S(1)} fusion(f32[4096]{0:T(1024)S(1)} %bitcast.133, s32[6144]{0:T(1024)S(1)} %broadcast_clamp_fusion), kind=kCustom, calls=%fused_computation.2 | custom fusion | bytes 73728 | tf_op jit(solution)/shard_map/gather | solution.py:101
  (86 shorter events, 15.3 us)
Async XLA Ops:
  7.2 80.6 %copy-start = (f32[32,32]{1,0:T(8,128)S(1)}, f32[32,32]{1,0:T(8,128)}, u32[]{:S(2)}) copy-start(f32[32,32]{1,0:T(8,128)} %param.21) | copy-start | bytes 12292
  7.2 0.8 copy-start.4
  7.2 59.7 %all-reduce.9.cloned.1.call-start = ((), (), s32[]{:S(2)}) async-start(), calls=%async_computation | async-start | bytes 163840
  9.2 0.7 copy-start.2
  12.4 0.7 copy-start.5
  13.0 6.6 %copy-start.1 = (f32[4,24,256]{2,1,0:T(8,128)S(1)}, f32[4,24,256]{2,1,0:T(8,128)}, u32[]{:S(2)}) copy-start(f32[4,24,256]{2,1,0:T(8,128)} %param.17) | copy-start | bytes 294916
  14.0 0.7 copy-start.7
  14.0 262.7 %all-reduce.11.cloned.1.call-start = ((), (), s32[]{:S(2)}) async-start(), calls=%async_computation.1 | async-start | bytes 163840
  14.7 73.0 %collective-permute-start = (f32[1,32,128]{2,1,0:T(8,128)S(1)}, f32[1,32,128]{2,1,0:T(8,128)S(1)}, u32[]{:S(2)}, u32[]{:S(2)}) collective-permute-start(f32[1,32,128]{2,1,0:T(8,128)S(1)} %copy-done.7), channel_id=1, source_target_pairs={{0,1},{1,2},{2,3},{3,4},{4,5},{5,6},{6,7},{7,8},{8,9},{9,10},{10,1... | collective-permute-start | bytes 49160 | tf_op jit(solution)/shard_map/ppermute | solution.py:14
  19.7 4.7 %collective-permute-start.1 = (f32[4,24,1]{2,1,0:T(8,128)S(1)}, f32[4,24,1]{2,1,0:T(8,128)S(1)}, u32[]{:S(2)}, u32[]{:S(2)}) collective-permute-start(f32[4,24,1]{2,1,0:T(8,128)S(1)} %get-tuple-element.104), channel_id=1, source_target_pairs={{1,0},{2,1},{3,2},{0,3},{5,4},{6,5},{7,6},{4,7},{9,8},{10,9},{11,1... | collective-permute-start | bytes 1160 | tf_op jit(solution)/shard_map/ppermute | solution.py:25
  21.7 6.4 %collective-permute-start.2 = (f32[4,24,1]{2,1,0:T(8,128)S(1)}, f32[4,24,1]{2,1,0:T(8,128)S(1)}, u32[]{:S(2)}, u32[]{:S(2)}) collective-permute-start(f32[4,24,1]{2,1,0:T(8,128)S(1)} %get-tuple-element.105), channel_id=1, source_target_pairs={{0,1},{1,2},{2,3},{3,0},{4,5},{5,6},{6,7},{7,4},{8,9},{9,10},{10,1... | collective-permute-start | bytes 1160 | tf_op jit(solution)/shard_map/ppermute | solution.py:24
  21.9 0.7 copy-start.10
  22.5 0.7 copy-start.9
  87.7 0.7 copy-start.6
  87.7 0.7 copy-start.8
  186.5 44.3 %collective-permute-start.4 = (f32[4,24,1]{2,1,0:T(8,128)S(1)}, f32[4,24,1]{2,1,0:T(8,128)S(1)}, u32[]{:S(2)}, u32[]{:S(2)}) collective-permute-start(f32[4,24,1]{2,1,0:T(8,128)S(1)} %get-tuple-element.99), channel_id=1, source_target_pairs={{1,0},{2,1},{3,2},{0,3},{5,4},{6,5},{7,6},{4,7},{9,8},{10,9},{11,1... | collective-permute-start | bytes 1160 | tf_op jit(solution)/shard_map/ppermute | solution.py:25
  187.0 43.9 %collective-permute-start.5 = (f32[4,24,1]{2,1,0:T(8,128)S(1)}, f32[4,24,1]{2,1,0:T(8,128)S(1)}, u32[]{:S(2)}, u32[]{:S(2)}) collective-permute-start(f32[4,24,1]{2,1,0:T(8,128)S(1)} %get-tuple-element.100), channel_id=1, source_target_pairs={{0,1},{1,2},{2,3},{3,0},{4,5},{5,6},{6,7},{7,4},{8,9},{9,10},{10,1... | collective-permute-start | bytes 1160 | tf_op jit(solution)/shard_map/ppermute | solution.py:24
  227.0 70.6 %collective-permute-start.3 = (f32[1,32,128]{2,1,0:T(8,128)S(1)}, f32[1,32,128]{2,1,0:T(8,128)S(1)}, u32[]{:S(2)}, u32[]{:S(2)}) collective-permute-start(f32[1,32,128]{2,1,0:T(8,128)S(1)} %bitcast.141), channel_id=1, source_target_pairs={{0,1},{1,2},{2,3},{3,4},{4,5},{5,6},{6,7},{7,8},{8,9},{9,10},{10,1... | collective-permute-start | bytes 49160 | tf_op jit(solution)/shard_map/ppermute | solution.py:14
  431.1 0.6 copy-start.3
Sparse Core Ops, SparseCore 0:
  14.1 52.7 all-reduce.8
  227.1 49.5 all-reduce.10
where the time goes:
time: 439 us
  blocking collectives  164 us (37%)
  local copies, waits for them, and re-layouts  147 us (33%)
  waiting for transfers between devices  88 us (20%)
  between operations  15.1 us (3%)
  starting transfers between devices  13.3 us (3%)
  matrix products  6.94 us (2%)
    all_gather x2, blocking collectives, body(): whole = lax.all_gather(table, ('sec', 'span'), axis=0, tiled=True)  127 us
    unnamed x4, waiting for transfers between devices  84.3 us
    gather x3, local copies, waits for them, and re-layouts, body(): rho_cell = whole[:, 0, :].reshape(-1)[index]  69.2 us
    gather x4, local copies, waits for them, and re-layouts, body(): temp_cell = whole[:, 1, :].reshape(-1)[index]  68.6 us
    unnamed x2, blocking collectives  37.3 us
    ppermute x2, starting transfers between devices, from_behind(): lax.ppermute(value, axis, [(source, source + steps) for source in range(f...  8.78 us
  transfers between devices with their start and end apart: 8, of which 3 were waited for; matrix products, arithmetic and copies ran while one was open for 10% of the time, Pallas kernels for 0%

commit v1 on v0

v1 whole, which is shorter than its diff:
```python
import functools

import jax
import jax.numpy as jnp
from jax import lax
from jax.experimental import pallas as pl
from jax.experimental.pallas import tpu as pltpu
from jax.sharding import PartitionSpec as P

MESH = pl.DeviceIdType.MESH
F32 = jnp.float32
BF16 = jnp.bfloat16
HIGH = lax.Precision.HIGHEST
NQ = 10
ROWS = 3


def split(x):
    hi = x.astype(BF16)
    return hi, (x - hi.astype(F32)).astype(BF16)


def iota(shape, dim):
    return lax.broadcasted_iota(jnp.int32, shape, dim)


def shifted(x, left, right):
    width = x.shape[1]
    lane = iota(x.shape, 1)
    down = jnp.where(lane == 0, left, pltpu.roll(x, 1, 1))
    up = jnp.where(lane == width - 1, right, pltpu.roll(x, width - 1, 1))
    return down, up


def lap_bins(x):
    down, up = shifted(x, 0.0, 0.0)
    return up + down - 2.0 * x


def kernel(
    n, J, PK,
    owner, invw, form, density, fields, bins, species, rate_m,
    sp_out, den_out, f_out,
    halo_out, halo_in, spin, vals, hist, send1, in1, sum1, send2, in2, sendp, inp, prevs,
    table, tabc,
    hsend, hrecv, ssend, srecv, send1s, recv1s, send2s, recv2s, sendps, recvps, tsend, trecv,
):
    C, Z = density.shape
    K, B = species.shape[1], species.shape[2]
    N = n * J
    i, j = lax.axis_index("sec"), lax.axis_index("span")
    s = i * J + j

    def dev(t):
        return (lax.div(t, J), lax.rem(t, J))

    barrier = pltpu.get_barrier_semaphore()

    @pl.loop(1, N)
    def _(d):
        pl.semaphore_signal(barrier, inc=1, device_id=dev(lax.rem(s + d, N)), device_id_type=MESH)

    lane = iota((C, 128), 1)
    binf = bins[...].astype(F32)
    first, last = binf[:, :128], binf[:, Z - 128:]
    to_left = jnp.where(lane == 8, pltpu.roll(first, 8, 1), 0.0)
    to_right = jnp.where(lane == 8, pltpu.roll(last, 9, 1), 0.0)
    for k in range(4):
        here = (lane == 2 * k) | (lane == 2 * k + 1)
        head, tail = fields[k, :, :128], fields[k, :, Z - 128:]
        if k:
            head = pltpu.roll(head, 2 * k, 1)
        to_left = jnp.where(here, head, to_left)
        to_right = jnp.where(here, pltpu.roll(tail, 2 * k + 2, 1), to_right)
    halo_out[0] = to_left
    halo_out[1] = to_right

    pl.semaphore_wait(barrier, N - 1)

    copies = []
    for side, step in ((0, J - 1), (1, 1)):
        copies.append(pltpu.make_async_remote_copy(
            halo_out.at[side], halo_in.at[side], hsend.at[side], hrecv.at[side],
            device_id=(i, lax.rem(j + step, J)), device_id_type=MESH))
    for step in (1, 2):
        copies.append(pltpu.make_async_remote_copy(
            species.at[0], spin.at[step - 1], ssend.at[step - 1], srecv.at[step - 1],
            device_id=dev(lax.rem(s + step, N)), device_id_type=MESH))
    for c in copies:
        c.start()

    den = density[...]

    def put(k, x):
        for h in range(Z // 128):
            vals[h, k * C:(k + 1) * C, :] = x[:, h * 128:(h + 1) * 128]

    put(0, den)
    put(5, jnp.ones((C, Z), F32))
    for k in range(4):
        f = fields[k]
        put(1 + k, den * f)
        down, up = shifted(f, 0.0, 0.0)
        put(6 + k, f + 0.2 * (down + up - 2.0 * f))
    for k in range(NQ, 16):
        put(k, jnp.zeros((C, Z), F32))

    bin_id = iota((B, Z), 0)
    for c in range(C):
        hot = jnp.where(bin_id == bins[c:c + 1, :], 1.0, 0.0).astype(BF16)
        v = jnp.concatenate([vals[h, pl.ds(c, 16, stride=C), :] for h in range(Z // 128)], axis=1)
        hi, lo = split(v)
        both = jnp.concatenate([hi, lo], axis=0)
        r = lax.dot_general(both, hot, (((1,), (1,)), ((), ())), preferred_element_type=F32)
        hist[c * 16:(c + 1) * 16, :] = r[:16] + r[16:]

    RT = PK * J
    R, PC = n * RT, PK * C
    G = -(-NQ // PK)
    q = iota((1, PC), 1)
    qc = lax.rem(q, C)
    own_lane = jnp.zeros((1, PC), jnp.int32)
    for c in range(C):
        own_lane = jnp.where(qc == c, owner[c], own_lane)
    r = iota((R, PC), 0)
    rem = lax.rem(r, RT)
    sec = lax.div(r, RT) * J + lax.rem(rem, J)
    same = lax.div(rem, J) == lax.div(iota((R, PC), 1), C)
    place = jnp.where(same & (sec == own_lane), 1.0, 0.0).astype(BF16)

    for c in copies[:2]:
        c.wait()
    from_left, from_right = halo_in[1], halo_in[0]
    lanes_b = iota((C, B), 1)
    bin_first, bin_last = bins[:, 0:1], bins[:, Z - 1:Z]
    hot_first = jnp.where(lanes_b == bin_first, 0.2, 0.0)
    hot_last = jnp.where(lanes_b == bin_last, 0.2, 0.0)

    def edge(tile, at):
        return tile[:, at:at + 1]

    slabs = []
    for k in range(G * PK):
        h = hist[pl.ds(k, C, stride=16), :]
        if 6 <= k < NQ:
            h = (h + hot_first * edge(from_left, 2 * (k - 6) + 1)
                 + hot_last * edge(from_right, 2 * (k - 6)))
        slabs.append(h)
    groups = []
    for g in range(G):
        part = slabs[g * PK:(g + 1) * PK]
        groups.append(part[0] if PK == 1 else jnp.concatenate(part, axis=0))
    wide = jnp.concatenate(groups, axis=1)
    hi, lo = split(wide)
    binned = (jnp.dot(place, hi, preferred_element_type=F32)
              + jnp.dot(place, lo, preferred_element_type=F32))
    for t in range(n):
        for g in range(G):
            send1[t, g * RT:(g + 1) * RT, :] = binned[t * RT:(t + 1) * RT, g * 128:(g + 1) * 128]

    outs1 = []
    for d in range(1, n):
        t = lax.rem(i + d, n)
        outs1.append(pltpu.make_async_remote_copy(
            send1.at[t], in1.at[d - 1], send1s, recv1s, device_id=(t, j), device_id_type=MESH))
    for c in outs1:
        c.start()

    for c in copies[2:]:
        c.wait()
    row = iota((K, B), 0)
    wcol = jnp.zeros((K, B), F32)
    fcol = jnp.zeros((K, B), F32)
    for k in range(K):
        wcol = jnp.where(row == k, invw[k], wcol)
        fcol = jnp.where(row == k, form[k], fcol)
    cur = species[0]
    prev = jnp.where(s >= 1, spin[0], 0.0)
    prev2 = jnp.where(s >= 2, spin[1], 0.0)
    rm = rate_m[...]
    rc = jnp.dot(rm, cur, precision=HIGH, preferred_element_type=F32)
    rp = jnp.dot(rm, prev, precision=HIGH, preferred_element_type=F32)
    rrc = jnp.dot(rm, rc, precision=HIGH, preferred_element_type=F32)
    lap_c, lap_p, lap_rc = lap_bins(cur), lap_bins(prev), lap_bins(rc)
    frc = jnp.sum(fcol * rc, axis=0, keepdims=True)

    lane256 = iota((C, Z), 1)
    ahead = []
    ends = []
    for k in range(4):
        f = fields[k]
        l2, l1 = edge(from_left, 2 * k), edge(from_left, 2 * k + 1)
        r1, r2 = edge(from_right, 2 * k), edge(from_right, 2 * k + 1)
        down, up = shifted(f, l1, r1)
        a = f + 0.2 * (down + up - 2.0 * f)
        al = l1 + 0.2 * (l2 + f[:, 0:1] - 2.0 * l1)
        ar = r1 + 0.2 * (r2 + f[:, Z - 1:Z] - 2.0 * r1)
        ahead.append(a)
        ends.append((al, ar))
        if k != 2:
            down, up = shifted(a, al, ar)
            f_out[k] = a + 0.2 * (down + up - 2.0 * a)

    pltpu.make_async_copy(in1, in1, recv1s).wait()
    total = send1[i]
    for d in range(n - 1):
        total = total + in1[d]
    sum1[...] = total
    for t in range(J):
        send2[t, 0:NQ, :] = sum1[pl.ds(t, NQ, stride=J), :]
        if t:
            send2[t, NQ:NQ + 5, :] = sum1[pl.ds(t - 1, 5, stride=J), :]
        else:
            send2[t, NQ:NQ + 5, :] = jnp.zeros((5, B), F32)
        send2[t, NQ + 5:16, :] = jnp.zeros((1, B), F32)
    sendp[0:5, :] = sum1[pl.ds(J - 1, 5, stride=J), :]
    sendp[5:8, :] = jnp.zeros((3, B), F32)
    outp = pltpu.make_async_remote_copy(
        sendp, inp.at[j], sendps, recvps, device_id=(lax.rem(i + 1, n), 0), device_id_type=MESH)
    outs2 = []
    for d in range(1, J):
        t = lax.rem(j + d, J)
        outs2.append(pltpu.make_async_remote_copy(
            send2.at[t], in2.at[d - 1], send2s, recv2s, device_id=(i, t), device_id_type=MESH))
    outp.start()
    for c in outs2:
        c.start()

    pltpu.make_async_copy(in2, in2, recv2s).wait()
    total = send2[j]
    for d in range(J - 1):
        total = total + in2[d]
    prevs[0:5, :] = total[NQ:NQ + 5]

    @pl.when(j == 0)
    def _():
        pltpu.make_async_copy(inp, inp, recvps).wait()
        tp = inp[0]
        for d in range(1, J):
            tp = tp + inp[d]
        prevs[...] = tp

    before_sums = prevs[...]
    eta = (iota((1, B), 1).astype(F32) + 0.5) / B
    base = 1.0 + 4.0 * eta * (1.0 - eta)

    def sigmoid(x):
        return 1.0 / (1.0 + jnp.exp(-x))

    def coeffs(w, qs):
        inv = 1.0 / jnp.maximum(w, 1.0)
        temp = base + 0.5 * jnp.tanh(qs[2] * inv)
        rate = jnp.exp(2.0 * (1.0 - 1.0 / temp))
        return temp, rate, 0.2 * sigmoid(qs[1] * inv), 0.3 * sigmoid(qs[0] * inv), 0.2 * sigmoid(qs[3] * inv)

    def line(x, k):
        return x[k:k + 1, :]

    temp, rate, mixing, carried, loss = coeffs(line(total, 0), [line(total, 1 + k) for k in range(4)])
    _, ratep, mixingp, carriedp, _ = coeffs(
        line(before_sums, 0), [line(before_sums, 1 + k) for k in range(4)])
    up0 = cur + mixing * lap_c - carried * (cur - prev) + 0.2 * (rc * rate)
    pp0 = prev + mixingp * lap_p - carriedp * (prev - prev2) + 0.2 * (rp * ratep)
    pp0 = jnp.where(s >= 1, pp0, 0.0)
    rup = rc + mixing * lap_rc - carried * (rc - rp) + 0.2 * (rate * rrc)
    rho0 = 1.0 / (temp * (1.0 + jnp.sum(wcol * up0 * up0, axis=0, keepdims=True) / K))
    tc0 = temp + 0.1 * (rate * frc) - loss * (temp - 0.5)

    count = line(total, 5)
    fs = [line(total, 6 + k) for k in range(4)]
    fs[2] = 0.7 * fs[2] + 0.3 * (tc0 * count)
    temp, rate, mixing, carried, loss = coeffs(rho0 * count, [rho0 * x for x in fs])
    react = rup * rate
    up1 = up0 + mixing * lap_bins(up0) - carried * (up0 - pp0) + 0.2 * react
    sp_out[0] = up1
    rho1 = 1.0 / (temp * (1.0 + jnp.sum(wcol * up1 * up1, axis=0, keepdims=True) / K))
    tc1 = temp + 0.1 * jnp.sum(fcol * react, axis=0, keepdims=True) - loss * (temp - 0.5)

    table[s, 0:1, :] = rho1
    table[s, 1:2, :] = tc0
    table[s, 2:3, :] = tc1

    mine = table.at[s, 0:ROWS]

    @pl.loop(1, N)
    def _(d):
        pltpu.make_async_remote_copy(
            mine, mine, tsend, trecv, device_id=dev(lax.rem(s + d, N)), device_id_type=MESH).start()

    pltpu.make_async_copy(in1, in1, send1s).wait()
    pltpu.make_async_copy(in2, in2, send2s).wait()
    outp.wait_send()
    some = table.at[0:N - 1, 0:ROWS]
    pltpu.make_async_copy(some, some, trecv).wait()

    for c in range(C):
        tabc[c * 8:c * 8 + ROWS, :] = table[owner[c], 0:ROWS, :]
    rho_col, t0_col, t1_col = (tabc[pl.ds(k, C, stride=8), :] for k in range(ROWS))

    def look(col, index):
        return jnp.take_along_axis(col, index, axis=1, mode="promise_in_bounds")

    def cells(col):
        return jnp.concatenate([look(col, bins[:, o:o + 128]) for o in range(0, Z, 128)], axis=1)

    den_out[...] = cells(rho_col)
    t0, t1 = cells(t0_col), cells(t1_col)
    t0_left = edge(look(t0_col, jnp.clip(from_left, 0.0, B - 1.0).astype(jnp.int32)), 8)
    t0_right = edge(look(t0_col, jnp.clip(from_right, 0.0, B - 1.0).astype(jnp.int32)), 8)
    a = ahead[2]
    a = a + 0.3 * (t0 - a)
    al, ar = ends[2]
    al = al + 0.3 * (t0_left - al)
    ar = ar + 0.3 * (t0_right - ar)
    down, up = shifted(a, al, ar)
    a = a + 0.2 * (down + up - 2.0 * a)
    f_out[2] = a + 0.3 * (t1 - a)
    pltpu.make_async_copy(some, some, tsend).wait()


def body(density, fields, bins, owner, species, rate_matrix, inv_weight, formation):
    n, J = lax.axis_size("sec"), lax.axis_size("span")
    C, Z = density.shape
    _, K, B = species.shape
    PK = max(1, 8 // J)
    G = -(-NQ // PK)
    T1 = G * PK * J
    vm = pl.BlockSpec(memory_space=pltpu.VMEM)
    sm = pl.BlockSpec(memory_space=pltpu.SMEM)
    dma = pltpu.SemaphoreType.DMA
    return pl.pallas_call(
        functools.partial(kernel, n, J, PK),
        out_shape=(
            jax.ShapeDtypeStruct(species.shape, F32),
            jax.ShapeDtypeStruct(density.shape, F32),
            jax.ShapeDtypeStruct(fields.shape, F32),
        ),
        in_specs=[sm, sm, sm, vm, vm, vm, vm, vm],
        out_specs=(vm, vm, vm),
        scratch_shapes=[
            pltpu.VMEM((2, C, 128), F32),
            pltpu.VMEM((2, C, 128), F32),
            pltpu.VMEM((2, K, B), F32),
            pltpu.VMEM((Z // 128, 16 * C, 128), F32),
            pltpu.VMEM((C * 16, B), F32),
            pltpu.VMEM((n, T1, B), F32),
            pltpu.VMEM((n - 1, T1, B), F32),
            pltpu.VMEM((T1, B), F32),
            pltpu.VMEM((J, 16, B), F32),
            pltpu.VMEM((J - 1, 16, B), F32),
            pltpu.VMEM((8, B), F32),
            pltpu.VMEM((J, 8, B), F32),
            pltpu.VMEM((8, B), F32),
            pltpu.VMEM((n * J, 8, B), F32),
            pltpu.VMEM((C * 8, B), F32),
            dma((2,)), dma((2,)), dma((2,)), dma((2,)),
            dma, dma, dma, dma, dma, dma, dma, dma,
        ],
        compiler_params=pltpu.CompilerParams(
            collective_id=0, has_side_effects=True, vmem_limit_bytes=32 * 2**20),
        name="coupling",
    )(owner, inv_weight, formation, density, fields, bins, species, rate_matrix)


def solution(mesh):
    return jax.shard_map(
        body,
        mesh=mesh,
        in_specs=(
            P("sec", "span"),
            P(None, "sec", "span"),
            P("sec", "span"),
            P("sec"),
            P(("sec", "span"), None, None),
            P(),
            P(),
            P(),
        ),
        out_specs=(P(("sec", "span"), None, None), P("sec", "span"), P(None, "sec", "span")),
        check_vma=False,
    )
```

time: 439 us -> 31.5 us (0.07)
  blocking collectives: 164 us -> 0 us
  local copies, waits for them, and re-layouts: 147 us -> 7.61 us
  waiting for transfers between devices: 88 us -> 0 us
  Pallas kernels: 0 us -> 22.8 us
  between operations: 15.1 us -> 0.66 us
  starting transfers between devices: 13.3 us -> 0 us
  matrix products: 6.94 us -> 0 us
    gather x7 -> x0, local copies, waits for them, and re-layouts: 138 us -> none  [the longest x3 69.2 us: body(): rho_cell = whole[:, 0, :].reshape(-1)[index]]
    all_gather x2 -> x0, blocking collectives: 127 us -> none  [body(): whole = lax.all_gather(table, ('sec', 'span'), axis=0, tiled=True)]
    unnamed x4 -> x0, waiting for transfers between devices: 84.3 us -> none
    unnamed x2 -> x0, blocking collectives: 37.3 us -> none
    pallas_call x0 -> x1, Pallas kernels: none -> 22.8 us  [body(): pl.pallas_call(functools.partial(kernel, n, J, PK), out_shape=(jax.ShapeD...]
    ppermute x6 -> x0, starting transfers between devices: 13.2 us -> none  [the longest x2 8.78 us: from_behind(): lax.ppermute(value, axis, [(source, source + steps) for source in range(f...]
    dot_general x10 -> x0, matrix products: 6.94 us -> none  [the longest x6 4.76 us: one_block(): jnp.einsum('cqz,czb->cqb', vals, hot, precision=lax.Precision.HIGHEST)]
  transfers between devices with their start and end apart: 8 -> 0, of which waited for: 3 -> 0; matrix products, arithmetic and copies ran while one was open for 10% -> 0% of each run, Pallas kernels for 0% -> 0%
where the time goes in v1:
time: 31.5 us; the launch traced here: 31 us
  Pallas kernels  22.8 us (72%)
  local copies, waits for them, and re-layouts  7.61 us (24%)
  between operations  0.66 us (2%)
    pallas_call x1, Pallas kernels, body(): pl.pallas_call(functools.partial(kernel, n, J, PK), out_shape=(jax.ShapeD...  22.8 us
    unnamed x19, local copies, waits for them, and re-layouts  7.61 us

profile of v1, /device:TPU:0, one launch (start us, length us, event | category | flops | bytes accessed | tf_op | source)
XLA Modules:
  0.0 31.0 jit_solution(5255398555262160684)
XLA Ops:
  0.6 0.0 copy-start
  0.6 0.9 %copy-done = f32[4,24,256]{2,1,0:T(8,128)S(1)} copy-done((f32[4,24,256]{2,1,0:T(8,128)S(1)}, f32[4,24,256]{2,1,0:T(8,128)}, u32[]{:S(2)}) %copy-start) | copy-done | bytes 98328
  1.5 0.0 copy-start.1
  1.5 0.7 %copy-done.1 = f32[24,256]{1,0:T(8,128)S(1)} copy-done((f32[24,256]{1,0:T(8,128)S(1)}, f32[24,256]{1,0:T(8,128)}, u32[]{:S(2)}) %copy-start.1) | copy-done | bytes 24600
  2.3 0.0 copy-start.2
  2.3 0.7 %copy-done.2 = s32[24,256]{1,0:T(8,128)S(1)} copy-done((s32[24,256]{1,0:T(8,128)S(1)}, s32[24,256]{1,0:T(8,128)}, u32[]{:S(2)}) %copy-start.2) | copy-done | bytes 24600
  3.0 0.0 copy-start.3
  3.0 0.7 %copy-done.3 = f32[1,32,128]{2,1,0:T(8,128)S(1)} copy-done((f32[1,32,128]{2,1,0:T(8,128)S(1)}, f32[1,32,128]{2,1,0:T(8,128)}, u32[]{:S(2)}) %copy-start.3) | copy-done | bytes 16408
  3.7 0.0 copy-start.4
  3.7 0.7 %copy-done.4 = f32[32,32]{1,0:T(8,128)S(1)} copy-done((f32[32,32]{1,0:T(8,128)S(1)}, f32[32,32]{1,0:T(8,128)}, u32[]{:S(2)}) %copy-start.4) | copy-done | bytes 4120
  4.4 0.0 copy-start.5
  4.4 0.7 %copy-done.5 = s32[24]{0:T(128)S(1)} copy-done((s32[24]{0:T(128)S(1)}, s32[24]{0:T(128)}, u32[]{:S(2)}) %copy-start.5) | copy-done | bytes 120
  5.1 0.0 copy-start.6
  5.1 0.7 %copy-done.6 = f32[32]{0:T(128)S(1)} copy-done((f32[32]{0:T(128)S(1)}, f32[32]{0:T(128)}, u32[]{:S(2)}) %copy-start.6) | copy-done | bytes 152
  5.8 0.0 copy-start.7
  5.8 0.7 %copy-done.7 = f32[32]{0:T(128)S(1)} copy-done((f32[32]{0:T(128)S(1)}, f32[32]{0:T(128)}, u32[]{:S(2)}) %copy-start.7) | copy-done | bytes 152
  6.4 22.8 %coupling.1 = (f32[1,32,128]{2,1,0:T(8,128)S(1)}, f32[24,256]{1,0:T(8,128)S(1)}, f32[4,24,256]{2,1,0:T(8,128)S(1)}) custom-call(s32[24]{0:T(128)S(1)} %copy-done.5, f32[32]{0:T(128)S(1)} %copy-done.6, f32[32]{0:T(128)S(1)} %copy-done.7, f32[24,256]{1,0:T(8,128)S(1)} %copy-done.1, f32[4,24,256]{2,1,0:T(8,128)S(1)} %copy-done, s32[24,256]{1,0:T(8,128)S(1)} %copy-done.2, ...), custom_call_target="tpu_custom_call" | custom-call | tf_op jit(solution)/shard_map/coupling/pallas_call | solution.py:331
  29.2 0.6 %copy.14 = f32[1,32,128]{2,1,0:T(8,128)} copy(f32[1,32,128]{2,1,0:T(8,128)S(1)} %get-tuple-element.6) | data formatting | bytes 32768
  29.8 0.6 %copy.15 = f32[24,256]{1,0:T(8,128)} copy(f32[24,256]{1,0:T(8,128)S(1)} %get-tuple-element.7) | data formatting | bytes 49152
  30.4 0.6 %copy.16 = f32[4,24,256]{2,1,0:T(8,128)} copy(f32[4,24,256]{2,1,0:T(8,128)S(1)} %get-tuple-element.8) | data formatting | bytes 196608
Async XLA Ops:
  0.6 0.9 %copy-start = (f32[4,24,256]{2,1,0:T(8,128)S(1)}, f32[4,24,256]{2,1,0:T(8,128)}, u32[]{:S(2)}) copy-start(f32[4,24,256]{2,1,0:T(8,128)} %fields.1) | copy-start | bytes 294916
  1.5 0.7 %copy-start.1 = (f32[24,256]{1,0:T(8,128)S(1)}, f32[24,256]{1,0:T(8,128)}, u32[]{:S(2)}) copy-start(f32[24,256]{1,0:T(8,128)} %density.1) | copy-start | bytes 73732
  2.3 0.7 %copy-start.2 = (s32[24,256]{1,0:T(8,128)S(1)}, s32[24,256]{1,0:T(8,128)}, u32[]{:S(2)}) copy-start(s32[24,256]{1,0:T(8,128)} %bins.1) | copy-start | bytes 73732
  3.0 0.7 %copy-start.3 = (f32[1,32,128]{2,1,0:T(8,128)S(1)}, f32[1,32,128]{2,1,0:T(8,128)}, u32[]{:S(2)}) copy-start(f32[1,32,128]{2,1,0:T(8,128)} %species.1) | copy-start | bytes 49156
  3.7 0.7 %copy-start.4 = (f32[32,32]{1,0:T(8,128)S(1)}, f32[32,32]{1,0:T(8,128)}, u32[]{:S(2)}) copy-start(f32[32,32]{1,0:T(8,128)} %rate_m.1) | copy-start | bytes 12292
  4.4 0.7 %copy-start.5 = (s32[24]{0:T(128)S(1)}, s32[24]{0:T(128)}, u32[]{:S(2)}) copy-start(s32[24]{0:T(128)} %owner.1) | copy-start | bytes 292
  5.1 0.7 %copy-start.6 = (f32[32]{0:T(128)S(1)}, f32[32]{0:T(128)}, u32[]{:S(2)}) copy-start(f32[32]{0:T(128)} %invw.1) | copy-start | bytes 388
  5.8 0.7 %copy-start.7 = (f32[32]{0:T(128)S(1)}, f32[32]{0:T(128)}, u32[]{:S(2)}) copy-start(f32[32]{0:T(128)} %form.1) | copy-start | bytes 388

commit v2 on v1

--- a/solution.py
+++ b/solution.py
@@ -39,8 +39,9 @@
 
 def kernel(
     n, J, PK,
-    owner, invw, form, density, fields, bins, species, rate_m,
+    owner_h, invw_h, form_h, density_h, fields_h, bins_h, species_h, rate_h,
     sp_out, den_out, f_out,
+    owner, invw, form, density, fields, bins, species, rate_m, loads,
     halo_out, halo_in, spin, vals, hist, send1, in1, sum1, send2, in2, sendp, inp, prevs,
     table, tabc,
     hsend, hrecv, ssend, srecv, send1s, recv1s, send2s, recv2s, sendps, recvps, tsend, trecv,
@@ -51,15 +52,27 @@
     i, j = lax.axis_index("sec"), lax.axis_index("span")
     s = i * J + j
 
+    def wrap(x, size):
+        return jnp.where(x >= size, x - size, x)
+
     def dev(t):
         return (lax.div(t, J), lax.rem(t, J))
 
+    pairs = ((fields_h, fields), (bins_h, bins), (density_h, density), (owner_h, owner),
+             (species_h, species), (rate_h, rate_m), (invw_h, invw), (form_h, form))
+    reads = [pltpu.make_async_copy(a, b, loads.at[k]) for k, (a, b) in enumerate(pairs)]
+    for c in reads:
+        c.start()
+
     barrier = pltpu.get_barrier_semaphore()
 
-    @pl.loop(1, N)
-    def _(d):
-        pl.semaphore_signal(barrier, inc=1, device_id=dev(lax.rem(s + d, N)), device_id_type=MESH)
-
+    for d in range(1, n):
+        pl.semaphore_signal(barrier, inc=1, device_id=(wrap(i + d, n), j), device_id_type=MESH)
+    for d in range(1, J):
+        pl.semaphore_signal(barrier, inc=1, device_id=(i, wrap(j + d, J)), device_id_type=MESH)
+
+    reads[0].wait()
+    reads[1].wait()
     lane = iota((C, 128), 1)
     binf = bins[...].astype(F32)
     first, last = binf[:, :128], binf[:, Z - 128:]
@@ -75,20 +88,23 @@
     halo_out[0] = to_left
     halo_out[1] = to_right
 
-    pl.semaphore_wait(barrier, N - 1)
+    pl.semaphore_wait(barrier, n + J - 2)
 
     copies = []
     for side, step in ((0, J - 1), (1, 1)):
         copies.append(pltpu.make_async_remote_copy(
             halo_out.at[side], halo_in.at[side], hsend.at[side], hrecv.at[side],
-            device_id=(i, lax.rem(j + step, J)), device_id_type=MESH))
+            device_id=(i, wrap(j + step, J)), device_id_type=MESH))
     for step in (1, 2):
         copies.append(pltpu.make_async_remote_copy(
-            species.at[0], spin.at[step - 1], ssend.at[step - 1], srecv.at[step - 1],
+            species_h.at[0], spin.at[step - 1], ssend.at[step - 1], srecv.at[step - 1],
             device_id=dev(lax.rem(s + step, N)), device_id_type=MESH))
-    for c in copies:
+    for c in copies[:2]:
         c.start()
-
+    for step in (1, 2):
+        pl.when(j + step < J)(copies[1 + step].start)
+
+    reads[2].wait()
     den = density[...]
 
     def put(k, x):
@@ -117,6 +133,7 @@
     RT = PK * J
     R, PC = n * RT, PK * C
     G = -(-NQ // PK)
+    reads[3].wait()
     q = iota((1, PC), 1)
     qc = lax.rem(q, C)
     own_lane = jnp.zeros((1, PC), jnp.int32)
@@ -160,13 +177,13 @@
 
     outs1 = []
     for d in range(1, n):
-        t = lax.rem(i + d, n)
+        t = wrap(i + d, n)
         outs1.append(pltpu.make_async_remote_copy(
             send1.at[t], in1.at[d - 1], send1s, recv1s, device_id=(t, j), device_id_type=MESH))
     for c in outs1:
         c.start()
 
-    for c in copies[2:]:
+    for c in reads[4:]:
         c.wait()
     row = iota((K, B), 0)
     wcol = jnp.zeros((K, B), F32)
@@ -175,13 +192,10 @@
         wcol = jnp.where(row == k, invw[k], wcol)
         fcol = jnp.where(row == k, form[k], fcol)
     cur = species[0]
-    prev = jnp.where(s >= 1, spin[0], 0.0)
-    prev2 = jnp.where(s >= 2, spin[1], 0.0)
     rm = rate_m[...]
     rc = jnp.dot(rm, cur, precision=HIGH, preferred_element_type=F32)
-    rp = jnp.dot(rm, prev, precision=HIGH, preferred_element_type=F32)
     rrc = jnp.dot(rm, rc, precision=HIGH, preferred_element_type=F32)
-    lap_c, lap_p, lap_rc = lap_bins(cur), lap_bins(prev), lap_bins(rc)
+    lap_c, lap_rc = lap_bins(cur), lap_bins(rc)
     frc = jnp.sum(fcol * rc, axis=0, keepdims=True)
 
     lane256 = iota((C, Z), 1)
@@ -216,15 +230,24 @@
     sendp[0:5, :] = sum1[pl.ds(J - 1, 5, stride=J), :]
     sendp[5:8, :] = jnp.zeros((3, B), F32)
     outp = pltpu.make_async_remote_copy(
-        sendp, inp.at[j], sendps, recvps, device_id=(lax.rem(i + 1, n), 0), device_id_type=MESH)
+        sendp, inp.at[j], sendps, recvps, device_id=(wrap(i + 1, n), 0), device_id_type=MESH)
     outs2 = []
     for d in range(1, J):
-        t = lax.rem(j + d, J)
+        t = wrap(j + d, J)
         outs2.append(pltpu.make_async_remote_copy(
             send2.at[t], in2.at[d - 1], send2s, recv2s, device_id=(i, t), device_id_type=MESH))
     outp.start()
     for c in outs2:
         c.start()
+
+    for step in (1, 2):
+        pl.when(j + step >= J)(copies[1 + step].start)
+    for c in copies[2:]:
+        c.wait()
+    prev = jnp.where(s >= 1, spin[0], 0.0)
+    prev2 = jnp.where(s >= 2, spin[1], 0.0)
+    rp = jnp.dot(rm, prev, precision=HIGH, preferred_element_type=F32)
+    lap_p = lap_bins(prev)
 
     pltpu.make_async_copy(in2, in2, recv2s).wait()
     total = send2[j]
@@ -282,10 +305,18 @@
 
     mine = table.at[s, 0:ROWS]
 
-    @pl.loop(1, N)
-    def _(d):
-        pltpu.make_async_remote_copy(
-            mine, mine, tsend, trecv, device_id=dev(lax.rem(s + d, N)), device_id_type=MESH).start()
+    def tell(d, first):
+        for e in range(first, J):
+            pltpu.make_async_remote_copy(
+                mine, mine, tsend, trecv, device_id=(wrap(i + d, n), wrap(j + e, J)),
+                device_id_type=MESH).start()
+
+    tell(0, 1)
+    if N <= 64:
+        for d in range(1, n):
+            tell(d, 0)
+    else:
+        pl.loop(1, n)(lambda d: tell(d, 0))
 
     pltpu.make_async_copy(in1, in1, send1s).wait()
     pltpu.make_async_copy(in2, in2, send2s).wait()
@@ -318,6 +349,15 @@
     pltpu.make_async_copy(some, some, tsend).wait()
 
 
+def store(a, b, c, a_out, b_out, c_out, sems):
+    copies = [pltpu.make_async_copy(x, y, sems.at[k])
+              for k, (x, y) in enumerate(((a, a_out), (b, b_out), (c, c_out)))]
+    for x in copies:
+        x.start()
+    for x in copies:
+        x.wait()
+
+
 def body(density, fields, bins, owner, species, rate_matrix, inv_weight, formation):
     n, J = lax.axis_size("sec"), lax.axis_size("span")
     C, Z = density.shape
@@ -326,18 +366,27 @@
     G = -(-NQ // PK)
     T1 = G * PK * J
     vm = pl.BlockSpec(memory_space=pltpu.VMEM)
-    sm = pl.BlockSpec(memory_space=pltpu.SMEM)
+    hbm = pl.BlockSpec(memory_space=pltpu.HBM)
     dma = pltpu.SemaphoreType.DMA
-    return pl.pallas_call(
+    results = pl.pallas_call(
         functools.partial(kernel, n, J, PK),
         out_shape=(
             jax.ShapeDtypeStruct(species.shape, F32),
             jax.ShapeDtypeStruct(density.shape, F32),
             jax.ShapeDtypeStruct(fields.shape, F32),
         ),
-        in_specs=[sm, sm, sm, vm, vm, vm, vm, vm],
+        in_specs=[hbm] * 8,
         out_specs=(vm, vm, vm),
         scratch_shapes=[
+            pltpu.SMEM(owner.shape, jnp.int32),
+            pltpu.SMEM(inv_weight.shape, F32),
+            pltpu.SMEM(formation.shape, F32),
+            pltpu.VMEM(density.shape, F32),
+            pltpu.VMEM(fields.shape, F32),
+            pltpu.VMEM(bins.shape, jnp.int32),
+            pltpu.VMEM(species.shape, F32),
+            pltpu.VMEM(rate_matrix.shape, F32),
+            dma((8,)),
             pltpu.VMEM((2, C, 128), F32),
             pltpu.VMEM((2, C, 128), F32),
             pltpu.VMEM((2, K, B), F32),
@@ -357,9 +406,17 @@
             dma, dma, dma, dma, dma, dma, dma, dma,
         ],
         compiler_params=pltpu.CompilerParams(
-            collective_id=0, has_side_effects=True, vmem_limit_bytes=32 * 2**20),
+            collective_id=0, has_side_effects=True),
         name="coupling",
     )(owner, inv_weight, formation, density, fields, bins, species, rate_matrix)
+    return pl.pallas_call(
+        store,
+        out_shape=tuple(jax.ShapeDtypeStruct(r.shape, F32) for r in results),
+        in_specs=[vm] * 3,
+        out_specs=(hbm,) * 3,
+        scratch_shapes=[dma((3,))],
+        name="store",
+    )(*results)
 
 
 def solution(mesh):

time: 31.5 us -> 25.2 us (0.80)
  local copies, waits for them, and re-layouts: 7.61 us -> 0 us
  Pallas kernels: 22.8 us -> 24.4 us
    unnamed x19 -> x0, local copies, waits for them, and re-layouts: 7.61 us -> none
    pallas_call x0 -> x1, Pallas kernels: none -> 1.61 us  [body(): pl.pallas_call(store, out_shape=tuple((jax.ShapeDtypeStruct(r.shape, F32)...]
where the time goes in v2:
time: 25.2 us; the launch traced here: 25 us
  Pallas kernels  24.4 us (97%)
  between operations  0.64 us (3%)
    pallas_call x1, Pallas kernels, body(): pl.pallas_call(functools.partial(kernel, n, J, PK), out_shape=(jax.ShapeD...  22.8 us
    pallas_call x1, Pallas kernels, body(): pl.pallas_call(store, out_shape=tuple((jax.ShapeDtypeStruct(r.shape, F32)...  1.61 us

profile of v2, /device:TPU:0, one launch (start us, length us, event | category | flops | bytes accessed | tf_op | source)
XLA Modules:
  0.0 25.0 jit_solution(1816156655403454163)
XLA Ops:
  0.6 22.8 %coupling.1 = (f32[1,32,128]{2,1,0:T(8,128)}, f32[24,256]{1,0:T(8,128)}, f32[4,24,256]{2,1,0:T(8,128)}) custom-call(s32[24]{0:T(128)} %owner_h.1, f32[32]{0:T(128)} %invw_h.1, f32[32]{0:T(128)} %form_h.1, f32[24,256]{1,0:T(8,128)} %density_h.1, f32[4,24,256]{2,1,0:T(8,128)} %fields_h.1, s32[24,256]{1,0:T(8,128)} %bins_h.1, f32[1,32,128]{2,1,0:T(8,128)} %species_h.1, ...), custom_call_target="tpu_custom_call" | custom-call | tf_op jit(solution)/shard_map/coupling/pallas_call | solution.py:371
  23.4 1.6 %store.1 = (f32[1,32,128]{2,1,0:T(8,128)}, f32[24,256]{1,0:T(8,128)}, f32[4,24,256]{2,1,0:T(8,128)}) custom-call(f32[1,32,128]{2,1,0:T(8,128)} %get-tuple-element.6.a, f32[24,256]{1,0:T(8,128)} %get-tuple-element.7.b, f32[4,24,256]{2,1,0:T(8,128)} %get-tuple-element.8.c), custom_call_target="tpu_custom_call" | custom-call | tf_op jit(solution)/shard_map/store/pallas_call | solution.py:412
